TPU v7x, 512 devices: a whole 4x4x16 slice. The times are simulated.
512 devices in a mesh: dp: 8 (over z_hi, x), context: 4 (over y), tensor: 16 (over z_lo, core).
Axes of the slice: x: 4, y: 4, z: 16 (z_hi: 2, z_lo: 8; z = z_hi * 8 + z_lo), core: 2. Of those that a mesh axis runs over, the one named last changes fastest.
Arguments:
- output_gradient: bfloat16 [8192, 4096], P(('dp', 'context', 'tensor')), may hold values from -6 to 6
- gate_preactivation: bfloat16 [8192, 16384], P(('dp', 'context'), 'tensor'), may hold values from -6 to 6
- up_preactivation: bfloat16 [8192, 16384], P(('dp', 'context'), 'tensor'), may hold values from -6 to 6
- router_scores_saved: float32 [8192, 8], P(('dp', 'context')), may hold values from -6 to 6
- router_input_rows: bfloat16 [8192, 4096], P(('dp', 'context', 'tensor')), may hold values from -6 to 6
- down_matrix: bfloat16 [16384, 4096], P('tensor', ('dp', 'context')), may hold values from -0.046875 to 0.046875
- adapter_first_factor: bfloat16 [16384, 512], P('tensor'), may hold values from -0.046875 to 0.046875
- adapter_second_factor: bfloat16 [512, 4096], P('tensor', ('dp', 'context')), may hold values from -0.25 to 0.25
Outputs:
- grad_gate: bfloat16 [8192, 16384], P(('dp', 'context'), 'tensor')
- grad_up: bfloat16 [8192, 16384], P(('dp', 'context'), 'tensor')
- router_grad: float32 [8, 4096], replicated
All inputs are finite; a program needn't handle non-finite values.
Results may differ from a plain program's by a relative error of at most 0.005.
Values may be sent and summed in bfloat16 or wider, within the bound.
A program may use at most 64 MiB of HBM per device.

v0:
```python
import math

import jax
import jax.numpy as jnp
from jax import lax
from jax.sharding import PartitionSpec as P


def local(
    output_gradient,
    gate_preactivation,
    up_preactivation,
    router_scores_saved,
    router_input_rows,
    down_matrix,
    adapter_first_factor,
    adapter_second_factor,
):
    tok_rows = gate_preactivation.shape[0]
    experts = router_scores_saved.shape[1]
    combined_rank = adapter_first_factor.shape[1]
    per_expert = combined_rank // experts
    tensor_pos = lax.axis_index("tensor")
    contracting_dimensions = (((1,), (1,)), ((), ()))
    full_grad = lax.all_gather(output_gradient, "tensor", axis=0, tiled=True)
    base_sum = lax.dot_general(
        full_grad,
        lax.all_gather(down_matrix, ("dp", "context"), axis=1, tiled=True),
        contracting_dimensions,
        preferred_element_type=jnp.float32,
    )
    low_sum = lax.dot_general(
        full_grad,
        lax.all_gather(adapter_second_factor, ("dp", "context"), axis=1, tiled=True),
        contracting_dimensions,
        preferred_element_type=jnp.float32,
    )
    grad_low_own = low_sum.astype(jnp.bfloat16)
    gate_vals = gate_preactivation.astype(jnp.float32)
    up_vals = up_preactivation.astype(jnp.float32)
    sigmoid_gate = jax.nn.sigmoid(gate_vals)
    hidden_state = (gate_vals * sigmoid_gate * up_vals).astype(jnp.bfloat16)
    gate_probs = jax.nn.sigmoid(router_scores_saved)
    rank_scale = jnp.broadcast_to(gate_probs[:, :, None], (tok_rows, experts, per_expert)).reshape(
        tok_rows, combined_rank
    )
    middle_portion = jnp.dot(hidden_state, adapter_first_factor, preferred_element_type=jnp.float32)
    middle_state = lax.psum(middle_portion, "tensor")
    lowrank_gradient = lax.all_gather(grad_low_own, "tensor", axis=1, tiled=True)
    low_vals = lowrank_gradient.astype(jnp.float32)
    grad_probs = (middle_state * low_vals).reshape(tok_rows, experts, per_expert).sum(-1)
    middle_gradient = (low_vals * rank_scale).astype(jnp.bfloat16)
    hidden_gradient = base_sum + lax.dot_general(
        middle_gradient,
        adapter_first_factor,
        contracting_dimensions,
        preferred_element_type=jnp.float32,
    )
    grad_up = (hidden_gradient * gate_vals * sigmoid_gate).astype(jnp.bfloat16)
    grad_gate = (
        hidden_gradient * up_vals * sigmoid_gate * (1.0 + gate_vals * (1.0 - sigmoid_gate))
    ).astype(jnp.bfloat16)
    grad_logits = grad_probs * gate_probs * (1.0 - gate_probs)
    rows_here = output_gradient.shape[0]
    own_logits = lax.dynamic_slice_in_dim(grad_logits, tensor_pos * rows_here, rows_here, 0)
    router_part = lax.dot_general(
        own_logits,
        router_input_rows.astype(jnp.float32),
        (((0,), (0,)), ((), ())),
        precision=lax.Precision.HIGHEST,
    )
    router_sum = lax.psum(router_part, ("dp", "context", "tensor"))
    tokens_total = tok_rows * lax.axis_size("dp") * lax.axis_size("context")
    router_grad = router_sum / math.sqrt(tokens_total)
    return (grad_gate, grad_up, router_grad)


def solution(mesh):
    return jax.shard_map(
        local,
        mesh=mesh,
        in_specs=(
            P(("dp", "context", "tensor"), None),
            P(("dp", "context"), "tensor"),
            P(("dp", "context"), "tensor"),
            P(("dp", "context"), None),
            P(("dp", "context", "tensor"), None),
            P("tensor", ("dp", "context")),
            P("tensor", None),
            P("tensor", ("dp", "context")),
        ),
        out_specs=(P(("dp", "context"), "tensor"), P(("dp", "context"), "tensor"), P()),
        check_vma=False,
    )
```

profile of v0, /device:TPU:1, one launch (start us, length us, event | category | flops | bytes accessed | tf_op | source)
XLA Modules:
  0.0 1005.7 jit_solution(11612469624964002486)
XLA Ops:
  8.0 0.0 copy-start
  8.0 0.0 all-gather.3.cloned.1.call-start
  8.1 0.7 all-gather.3.cloned.1.call-update
  8.7 0.0 copy-start.5
  8.8 0.0 copy-start.4
  8.8 0.0 all-reduce.3.cloned.1.call-start
  8.8 0.4 copy-done
  9.2 2.7 fusion.11
  11.9 0.0 copy-start.3
  11.9 0.0 all-reduce.3.cloned.1.call-update
  12.0 0.0 all-reduce.5.cloned.1.call-start
  12.0 0.0 copy-done.5
  12.0 0.0 copy-done.4
  12.1 152.1 %all_gather.14 = bf16[32,4096]{1,0:T(8,128)(2,1)S(1)} all-gather(bf16[32,128]{1,0:T(8,128)(2,1)S(1)} %copy-done.4), channel_id=1, replica_groups=mesh['dp'=8,'context'=4,'tensor'=16] {'dp','context'}, dimensions={1}, use_global_device_ids=true | all-gather | bytes 270336 | tf_op jit(solution)/shard_map/all_gather | solution.py:34
  164.1 0.0 all-gather.3.cloned.1.call-done
  164.1 0.0 copy-start.1
  164.1 2.5 convolution_convert_fusion
  166.6 44.7 %all_gather.15 = bf16[256,512]{0,1:T(8,128)(2,1)S(1)} all-gather(bf16[256,32]{0,1:T(8,128)(2,1)S(1)} %convolution_convert_fusion), channel_id=1, replica_groups=mesh['dp'=8,'context'=4,'tensor'=16] {'tensor'}, dimensions={1}, use_global_device_ids=true | all-gather | bytes 278528 | tf_op jit(solution)/shard_map/all_gather | solution.py:49
  211.3 107.0 %all-reduce.3.cloned.1.call-done = f32[256,512]{0,1:T(8,128)} async-done(((f32[256,512]{0,1:T(8,128)}), f32[256,512]{0,1:T(8,128)}) %all-reduce.3.cloned.1.call-update) | async-done | bytes 524304 | tf_op jit(solution)/shard_map/psum | solution.py:48
  318.3 1.1 bitcast_reduce_fusion
  319.5 0.0 copy-done.3
  319.5 0.9 fusion.14
  320.4 0.0 all-reduce.5.cloned.1.call-update
  320.4 0.0 all-gather.5.cloned.1.call-start
  320.5 0.5 all-gather.5.cloned.1.call-update
  321.0 0.8 fusion.10
  321.8 667.6 %all-reduce.5.cloned.1.call-done = f32[8,4096]{1,0:T(8,128)} async-done(((f32[8,4096]{1,0:T(8,128)}), f32[8,4096]{1,0:T(8,128)}) %all-reduce.5.cloned.1.call-update) | async-done | bytes 131088 | tf_op jit(solution)/shard_map/psum | solution.py:72
  989.4 1.6 broadcast_multiply_fusion
  990.9 0.0 copy-start.2
  990.9 0.0 all-gather.5.cloned.1.call-done
  990.9 0.0 copy-done.1
  990.9 0.0 copy-start.6
  991.0 0.0 copy-start.7
  991.0 5.8 fusion.22
  996.8 0.0 copy-done.2
  996.8 0.0 copy-done.6
  996.8 0.0 copy-done.7
  996.8 1.8 fusion.9
  (1 shorter events, 0.0 us)
Async XLA Ops:
  8.0 1.2 copy-start
  8.0 156.1 %all-gather.3.cloned.1.call-start = ((), (), s32[]{:S(2)}) async-start(), calls=%async_computation | async-start | bytes 2228224 | tf_op jit(solution)/shard_map/all_gather | solution.py:25
  8.7 3.3 copy-start.5
  8.8 3.3 copy-start.4
  8.8 309.5 %all-reduce.3.cloned.1.call-start = ((), (), s32[]{:S(2)}) async-start(), calls=%async_computation.2 | async-start | bytes 1048576 | tf_op jit(solution)/shard_map/psum | solution.py:48
  11.9 307.5 %copy-start.3 = (bf16[16,4096]{1,0:T(8,128)(2,1)S(1)}, bf16[16,4096]{1,0:T(8,128)(2,1)}, u32[]{:S(2)}) copy-start(bf16[16,4096]{1,0:T(8,128)(2,1)} %param.12) | copy-start | bytes 393220
  12.0 977.4 %all-reduce.5.cloned.1.call-start = ((), (), s32[]{:S(2)}) async-start(), calls=%async_computation.3 | async-start | bytes 262144 | tf_op jit(solution)/shard_map/psum | solution.py:72
  164.1 826.8 %copy-start.1 = (bf16[256,4096]{1,0:T(8,128)(2,1)S(1)}, bf16[256,4096]{1,0:T(8,128)(2,1)}, u32[]{:S(2)}) copy-start(bf16[256,4096]{1,0:T(8,128)(2,1)} %all-gather.3.cloned.1.call-done) | copy-start | bytes 6291460
  320.4 670.5 %all-gather.5.cloned.1.call-start = ((), (), s32[]{:S(2)}) async-start(), calls=%async_computation.1 | async-start | bytes 8650752 | tf_op jit(solution)/shard_map/all_gather | solution.py:28
  990.9 5.9 copy-start.2
  990.9 5.9 copy-start.6
  991.0 5.9 copy-start.7
Sparse Core Ops, SparseCore 0:
  10.9 106.3 all-gather.2
  120.8 197.4 all-reduce.2
  325.2 664.0 all-reduce.4
Sparse Core Ops, SparseCore 1:
  325.0 323.8 all-gather.4
where the time goes:
time: 1010 us
  waiting for transfers between devices  776 us (77%)
  blocking collectives  197 us (20%)
  between operations  15.3 us (2%)
  matrix products  13.7 us (1%)
    psum x1, waiting for transfers between devices, local(): router_sum = lax.psum(router_part, ('dp', 'context', 'tensor'))  668 us
    all_gather x1, blocking collectives, local(): lax.all_gather(adapter_second_factor, ('dp', 'context'), axis=1, tiled=True)  152 us
    psum x1, waiting for transfers between devices, local(): middle_state = lax.psum(middle_portion, 'tensor')  107 us
    all_gather x1, blocking collectives, local(): lax.all_gather(grad_low_own, 'tensor', axis=1, tiled=True)  44.7 us
  transfers between devices with their start and end apart: 4, of which 2 were waited for; matrix products, arithmetic and copies ran while one was open for 1% of the time, Pallas kernels for 0%

commit v1 on v0

v1 whole, which is shorter than its diff:
```python
import math

import jax
import jax.numpy as jnp
from jax import lax
from jax.experimental import pallas as pl
from jax.experimental.pallas import tpu as pltpu
from jax.sharding import PartitionSpec as P

MESH = pl.DeviceIdType.MESH
NT = (((1,), (1,)), ((), ()))
BF = jnp.bfloat16
F32 = jnp.float32
HI = lax.Precision.HIGHEST
QORDER = (0, 2, 1, 3)


def iota(shape, dim):
    return lax.broadcasted_iota(jnp.int32, shape, dim)


def kernel(
    scale,
    og_ref, gate_ref, up_ref, scores_ref, rows_ref, down_ref, first_ref, second_ref,
    gg_ref, gu_ref, rg_ref,
    wb, gb, a2b, gate, up, first, rows, hid, su, sg, mid, rs, pr, acc, lowb,
    qs, qs_in, qo, qr, rpb, rs_in, t1, rx, t2, ry, rz, fin,
    in_sem, w_send, w_recv, wz_recv,
    g_send, gsib_send, g_recv, gsib_recv,
    a2_send, a2z_recv, a2y_recv, a2x_recv,
    low_send, low_recv, q_send, q_recv,
    r_send, rs_recv, rx_recv, ry_recv, rz_recv, ay_recv, ax_recv, as_recv,
):
    dp = lax.axis_index("dp")
    y = lax.axis_index("context")
    ten = lax.axis_index("tensor")
    zh, x = dp // 4, dp % 4
    zl, c = ten // 2, ten % 2
    z = zh * 8 + zl
    oc = 1 - c

    def at_x(d):
        return (zh * 4 + (x + d + 4) % 4, y, ten)

    def at_y(d):
        return (dp, (y + d + 4) % 4, ten)

    def at_z(d):
        zz = (z + d + 16) % 16
        return ((zz // 8) * 4 + x, y, (zz % 8) * 2 + c)

    def at_zl(l):
        return (dp, y, l * 2 + c)

    sibling = (dp, y, zl * 2 + oc)

    def rc(src, dst, ss, rsm, dev):
        return pltpu.make_async_remote_copy(
            src_ref=src, dst_ref=dst, send_sem=ss, recv_sem=rsm, device_id=dev, device_id_type=MESH
        )

    def arrived(ref, sem):
        rc(ref, ref, w_send, sem, sibling).wait_recv()

    def sent(ref, sem):
        rc(ref, ref, sem, as_recv, sibling).wait_send()

    own_slot = (zh * 4 + x) * 4 + y
    my_rows = pl.ds(pl.multiple_of(ten * 16, 16), 16)

    ins = [
        pltpu.make_async_copy(og_ref, gb.at[my_rows], in_sem.at[0]),
        pltpu.make_async_copy(down_ref, wb.at[own_slot], in_sem.at[1]),
        pltpu.make_async_copy(second_ref, a2b.at[own_slot], in_sem.at[2]),
        pltpu.make_async_copy(gate_ref, gate, in_sem.at[3]),
        pltpu.make_async_copy(up_ref, up, in_sem.at[4]),
        pltpu.make_async_copy(first_ref, first, in_sem.at[5]),
        pltpu.make_async_copy(rows_ref, rows, in_sem.at[6]),
    ]
    for cp in ins:
        cp.start()

    peers = [sibling] + [at_x(d) for d in (1, 2, 3)] + [at_y(d) for d in (1, 2, 3)]
    peers += [at_z(d) for d in range(1, 16)]
    barrier = pltpu.get_barrier_semaphore()
    for dev in peers:
        pl.semaphore_signal(barrier, inc=1, device_id=dev, device_id_type=MESH)

    ins[3].wait()
    ins[4].wait()

    @pl.loop(0, 8)
    def _(i):
        r = pl.ds(pl.multiple_of(i * 32, 32), 32)
        g = gate[r, :].astype(F32)
        u = up[r, :].astype(F32)
        s = jax.nn.sigmoid(g)
        gs = g * s
        hid[r, :] = (gs * u).astype(BF)
        su[r, :] = gs
        sg[r, :] = u * s * (1.0 + g * (1.0 - s))

    ins[0].wait()
    ins[1].wait()
    ins[2].wait()
    pl.semaphore_wait(barrier, len(peers))

    def g_part(l, core, h):
        return gb.at[pl.ds(pl.multiple_of((l * 2 + core) * 16, 16), 16), pl.ds(h * 2048, 2048)]

    def g_block(l, core):
        return gb.at[pl.ds(pl.multiple_of((l * 2 + core) * 16, 16), 16)]

    def g_forward(l, h, to):
        rc(g_part(l, c, h), g_part(l, c, h), g_send, g_recv.at[l * 2 + h], at_zl(to)).start()

    def g_sibling(l):
        rc(g_block(l, c), g_block(l, c), gsib_send, gsib_recv.at[l], sibling).start()

    for h in range(2):
        @pl.when(zl < 7)
        def _():
            g_forward(zl, h, zl + 1)

        @pl.when(zl > 0)
        def _():
            g_forward(zl, h, zl - 1)

    def a2_y(zz):
        for d in (1, 2, 3):
            slot = (zz * 4 + x) * 4 + y
            rc(a2b.at[slot], a2b.at[slot], a2_send, a2y_recv.at[zz * 4 + y], at_y(d)).start()

    def a2_x(zz):
        for d in (1, 2, 3):
            slot = (zz * 4 + (x + d) % 4) * 4
            yy = (y + d) % 4
            arrived(a2b.at[(zz * 4 + x) * 4 + yy], a2y_recv.at[zz * 4 + yy])
        four = a2b.at[pl.ds((zz * 4 + x) * 4, 4)]
        for d in (1, 2, 3):
            rc(four, four, a2_send, a2x_recv.at[zz * 4 + x], at_x(d)).start()

    def a2_done(zz):
        for d in (1, 2, 3):
            xx = (x + d) % 4
            arrived(a2b.at[pl.ds((zz * 4 + xx) * 4, 4)], a2x_recv.at[zz * 4 + xx])

    zo = 1 - zh
    oth_slot = (zo * 4 + x) * 4 + y
    rc(a2b.at[own_slot], a2b.at[own_slot], a2_send, a2z_recv, at_z(8)).start()
    a2_y(zh)

    def w_part(slot, q):
        return wb.at[slot, pl.ds(q * 256, 256)]

    def place(zz, q, da, db):
        xx, yy = (x + da, y + db) if q < 2 else (x + db, y + da)
        return (zz * 4 + (xx + 4) % 4) * 4 + (yy + 4) % 4

    def w_send_to(slot, q, along, d):
        first_axis_x = q < 2
        dev = at_x(d) if (along == 0) == first_axis_x else at_y(d)
        rc(w_part(slot, q), w_part(slot, q), w_send, w_recv.at[slot * 4 + q], dev).start()

    def w_wait(slot, q):
        arrived(w_part(slot, q), w_recv.at[slot * 4 + q])

    def e0(zz, q):
        s = place(zz, q, 0, 0)
        w_send_to(s, q, 0, 1)
        w_send_to(s, q, 0, -1)
        w_send_to(s, q, 1, 1)
        w_send_to(s, q, 1, -1)

    def e1(zz, q):
        for da in (-1, 1):
            s = place(zz, q, da, 0)
            w_wait(s, q)
            if da == (-1 if q % 2 == 0 else 1):
                w_send_to(s, q, 0, -da)
            w_send_to(s, q, 1, 1)
            w_send_to(s, q, 1, -1)

    def e2(zz, q):
        s = place(zz, q, 2, 0)
        w_wait(s, q)
        w_send_to(s, q, 1, 1)
        w_send_to(s, q, 1, -1)

    def e3(zz, q, das):
        for da in das:
            for db in (-1, 1):
                s = place(zz, q, da, db)
                w_wait(s, q)
                if db == (-1 if q % 2 == 0 else 1):
                    w_send_to(s, q, 1, -db)

    def e4(zz, q):
        for da in (0, -1, 1, 2):
            w_wait(place(zz, q, da, 2), q)

    for q in QORDER:
        e0(zh, q)
    g_sibling(zl)
    for q in QORDER:
        rc(w_part(own_slot, q), w_part(own_slot, q), w_send, wz_recv.at[q], at_z(8)).start()

    p = jax.nn.sigmoid(scores_ref[...])
    lane = iota((256, 512), 1) // 64
    scale_rows = jnp.broadcast_to(p[:, 0:1], (256, 512))
    for e in range(1, 8):
        scale_rows = jnp.where(lane == e, p[:, e : e + 1], scale_rows)
    rs[...] = scale_rows
    lane = iota((256, 128), 1) // 16
    p16 = jnp.broadcast_to(p[:, 0:1], (256, 128))
    for e in range(1, 8):
        p16 = jnp.where(lane == e, p[:, e : e + 1], p16)
    same = iota((256, 128), 0) % 16 == iota((256, 128), 1) % 16
    pr[...] = jnp.where(same, p16 * (1.0 - p16), 0.0)
    ins[5].wait()
    ins[6].wait()

    def g_step(s):
        for sign in (-1, 1):
            l = zl + sign * s
            ok = (l >= 0) if sign < 0 else (l <= 7)
            more = (zl < 7) if sign < 0 else (zl > 0)

            @pl.when(ok)
            def _():
                for h in range(2):
                    arrived(g_part(l, c, h), g_recv.at[l * 2 + h])

                    @pl.when(more)
                    def _():
                        g_forward(l, h, zl - sign)
                g_sibling(l)

    for q in QORDER:
        e1(zh, q)
    g_step(1)
    a2_x(zh)
    for q in QORDER:
        e3(zh, q, (0,))
    g_step(2)
    for q in QORDER:
        e2(zh, q)
    g_step(3)
    arrived(a2b.at[oth_slot], a2z_recv)
    a2_y(zo)
    for q in QORDER:
        e3(zh, q, (-1, 1))
    for n in range(2):
        mid[:, 256 * n : 256 * n + 256] = jnp.dot(
            hid[...], first[:, 256 * n : 256 * n + 256], preferred_element_type=F32
        )
    g_step(4)
    a2_x(zo)
    for q in QORDER:
        e3(zh, q, (2,))
    g_step(5)
    a2_done(zh)
    g_step(6)
    a2_done(zo)
    g_step(7)

    def z_in(q):
        arrived(w_part(oth_slot, q), wz_recv.at[q])
        e0(zo, q)

    z_in(0)
    z_in(2)

    for d in range(8):
        arrived(g_block(d, oc), gsib_recv.at[d])

    def low_group(i, tot):
        a = jnp.concatenate([a2b[i * 4 + k] for k in range(4)], axis=1)
        g = gb[:, pl.ds(pl.multiple_of(i * 512, 512), 512)]
        return tot + lax.dot_general(a, g, NT, preferred_element_type=F32)

    lowb[ten] = lax.fori_loop(0, 8, low_group, jnp.zeros((32, 256), F32)).astype(BF)

    def low_out(j, dev):
        rc(lowb.at[j], lowb.at[j], low_send, low_recv.at[j], dev).start()

    for d in range(1, 8):
        low_out(ten, at_zl((zl + d) % 8))
    low_out(ten, sibling)

    z_in(1)
    z_in(3)
    for q in QORDER:
        e4(zh, q)

    def base_tile(zz, n):
        tot = None
        for k in range(4):
            w = jnp.concatenate(
                [wb[zz * 16 + k * 4 + i, pl.ds(pl.multiple_of(n * 256, 256), 256), :] for i in range(4)], axis=1
            )
            g = gb[:, pl.ds(pl.multiple_of(zz * 2048 + k * 512, 512), 512)]
            t = lax.dot_general(g, w, NT, preferred_element_type=F32)
            tot = t if tot is None else tot + t
        return tot

    @pl.loop(0, 4)
    def _(n):
        acc[:, pl.ds(pl.multiple_of(n * 256, 256), 256)] = base_tile(zh, n)

    for q in (0, 2):
        e1(zo, q)
    for d in range(1, 8):
        j = ((zl + d) % 8) * 2 + c
        arrived(lowb.at[j], low_recv.at[j])
        low_out(j, sibling)
    for q in (1, 3):
        e1(zo, q)
    for q in QORDER:
        e3(zo, q, (0,))
    for d in range(8):
        j = d * 2 + oc
        arrived(lowb.at[j], low_recv.at[j])

    low = jnp.transpose(lowb[...].reshape(512, 256).astype(F32))
    pm = mid[...] * low
    spread = jnp.where(iota((512, 128), 0) // 64 == iota((512, 128), 1) // 16, 1.0, 0.0)
    part = jnp.dot(pm, spread, precision=HI, preferred_element_type=F32) * pr[...]
    pick = jnp.where(iota((16, 256), 1) // 16 == iota((16, 256), 0), 1.0, 0.0)
    qs[...] = jnp.dot(pick, part, precision=HI, preferred_element_type=F32)
    rc(qs, qs_in, q_send.at[0], q_recv.at[8], sibling).start()
    hid[:, 0:512] = (low * rs[...]).astype(BF)

    for q in QORDER:
        e2(zo, q)
    arrived(qs_in, q_recv.at[8])
    both = qs[...] + qs_in[...]
    for l in range(8):
        row = jnp.where(c == 0, both[2 * l : 2 * l + 1], both[2 * l + 1 : 2 * l + 2])
        qo[l] = jnp.broadcast_to(row, (8, 128))
    qr[zl] = qo[zl]
    for d in range(1, 8):
        l = (zl + d) % 8
        rc(qo.at[l], qr.at[zl], q_send.at[1], q_recv.at[zl], at_zl(l)).start()

    for n in range(4):
        acc[:, 256 * n : 256 * n + 256] += lax.dot_general(
            hid[:, 0:512], first[256 * n : 256 * n + 256, :], NT, preferred_element_type=F32
        )
    for q in QORDER:
        e3(zo, q, (-1, 1))

    for d in range(1, 8):
        l = (zl + d) % 8
        arrived(qr.at[l], q_recv.at[l])
    lsum = qr[0]
    for l in range(1, 8):
        lsum = lsum + qr[l]
    lmat = jnp.where(iota((8, 128), 0) == iota((8, 128), 1) // 16, lsum, 0.0)
    fold = jnp.where(iota((128, 16), 0) % 16 == iota((128, 16), 1), 1.0, 0.0)
    l2 = jnp.dot(lmat, fold, precision=HI, preferred_element_type=F32)
    for k in range(4):
        t = jnp.dot(l2, rows[:, 1024 * k : 1024 * k + 1024].astype(F32), precision=HI, preferred_element_type=F32)
        for i in range(8):
            rpb[k * 8 + i] = t[:, 128 * i : 128 * i + 128]
    rc(rpb.at[pl.ds(oc * 16, 16)], rs_in, r_send.at[0], rs_recv, sibling).start()
    for q in QORDER:
        e3(zo, q, (2,))
    arrived(rs_in, rs_recv)
    t1[...] = rpb[pl.ds(c * 16, 16)] + rs_in[...]
    for d in (1, 2, 3):
        rc(t1.at[pl.ds(((x + d) % 4) * 4, 4)], rx.at[x], r_send.at[1], rx_recv.at[x], at_x(d)).start()
    rx[x] = t1[pl.ds(x * 4, 4)]
    for d in (1, 2, 3):
        xx = (x + d) % 4
        arrived(rx.at[xx], rx_recv.at[xx])
    t2[...] = rx[0] + rx[1] + rx[2] + rx[3]
    for d in (1, 2, 3):
        rc(t2.at[(y + d) % 4], ry.at[y], r_send.at[2], ry_recv.at[y], at_y(d)).start()
    ry[y] = t2[y]
    for d in (1, 2, 3):
        yy = (y + d) % 4
        arrived(ry.at[yy], ry_recv.at[yy])
    rz[z] = ry[0] + ry[1] + ry[2] + ry[3]
    for d in range(1, 16):
        rc(rz.at[z], rz.at[z], r_send.at[3], rz_recv.at[z], at_z(d)).start()

    for q in range(4):
        e4(zo, q)
        cols = slice(256 * q, 256 * q + 256)
        hg = acc[:, cols] + base_tile(zo, q)
        gu_ref[:, cols] = (hg * su[:, cols]).astype(BF)
        gg_ref[:, cols] = (hg * sg[:, cols]).astype(BF)

    for d in range(1, 16):
        zz = (z + d) % 16
        arrived(rz.at[zz], rz_recv.at[zz])
    tot = rz[0]
    for l in range(1, 16):
        tot = tot + rz[l]
    piece = c * 16 + x * 4 + y
    fin[piece] = tot / scale
    for d in (1, 2, 3):
        rc(fin.at[piece], fin.at[piece], r_send.at[4], ay_recv.at[y], at_y(d)).start()
    for d in (1, 2, 3):
        yy = (y + d) % 4
        arrived(fin.at[c * 16 + x * 4 + yy], ay_recv.at[yy])
    four = fin.at[pl.ds(c * 16 + x * 4, 4)]
    for d in (1, 2, 3):
        rc(four, four, r_send.at[5], ax_recv.at[x], at_x(d)).start()
    for d in (1, 2, 3):
        xx = (x + d) % 4
        arrived(fin.at[pl.ds(c * 16 + xx * 4, 4)], ax_recv.at[xx])
    half = fin.at[pl.ds(c * 16, 16)]
    rc(half, half, r_send.at[6], as_recv, sibling).start()
    arrived(fin.at[pl.ds(oc * 16, 16)], as_recv)
    for i in range(32):
        rg_ref[:, 128 * i : 128 * i + 128] = fin[i]

    sent(wb.at[pl.ds(0, 31)], w_send)
    sent(gb.at[pl.ds(0, 128)], gsib_send)
    inner = jnp.logical_and(zl > 0, zl < 7)

    @pl.when(inner)
    def _():
        sent(gb.at[pl.ds(0, 144)], g_send)

    @pl.when(jnp.logical_not(inner))
    def _():
        sent(gb.at[pl.ds(0, 16)], g_send)

    sent(a2b.at[pl.ds(0, 31)], a2_send)
    sent(lowb.at[pl.ds(0, 15)], low_send)
    sent(qs, q_send.at[0])
    sent(qo.at[pl.ds(0, 7)], q_send.at[1])
    for i, n in enumerate((16, 12, 3, 15, 3, 12, 16)):
        sent(rpb.at[pl.ds(0, n)], r_send.at[i])


def local(og, gate, up, scores, rows, down, first, second):
    tokens = gate.shape[0] * lax.axis_size("dp") * lax.axis_size("context")
    anywhere = pl.BlockSpec(memory_space=pl.ANY)
    vmem = pl.BlockSpec(memory_space=pltpu.VMEM)
    dma = pltpu.SemaphoreType.DMA
    V = pltpu.VMEM

    def body(*refs):
        kernel(math.sqrt(tokens), *refs)

    return pl.pallas_call(
        body,
        out_shape=(
            jax.ShapeDtypeStruct((256, 1024), BF),
            jax.ShapeDtypeStruct((256, 1024), BF),
            jax.ShapeDtypeStruct((8, 4096), F32),
        ),
        in_specs=[anywhere, anywhere, anywhere, vmem, anywhere, anywhere, anywhere, anywhere],
        out_specs=(vmem, vmem, vmem),
        scratch_shapes=[
            V((32, 1024, 128), BF), V((256, 4096), BF), V((32, 32, 128), BF),
            V((256, 1024), BF), V((256, 1024), BF), V((1024, 512), BF), V((16, 4096), BF),
            V((256, 1024), BF), V((256, 1024), F32), V((256, 1024), F32), V((256, 512), F32),
            V((256, 512), F32), V((256, 128), F32), V((256, 1024), F32), V((16, 32, 256), BF),
            V((16, 128), F32), V((16, 128), F32), V((8, 8, 128), F32), V((8, 8, 128), F32),
            V((32, 8, 128), F32), V((16, 8, 128), F32), V((16, 8, 128), F32), V((4, 4, 8, 128), F32),
            V((4, 8, 128), F32), V((4, 8, 128), F32), V((16, 8, 128), F32), V((32, 8, 128), F32),
            dma((7,)), dma, dma((128,)), dma((4,)),
            dma, dma, dma((16,)), dma((8,)),
            dma, dma, dma((8,)), dma((8,)),
            dma, dma((16,)), dma((2,)), dma((9,)),
            dma((7,)), dma, dma((4,)), dma((4,)), dma((16,)), dma((4,)), dma((4,)), dma,
        ],
        compiler_params=pltpu.CompilerParams(
            collective_id=0, has_side_effects=True, vmem_limit_bytes=48 * 2**20
        ),
        cost_estimate=pl.CostEstimate(flops=3 * 10**9, bytes_accessed=4 * 2**20, transcendentals=2**18),
        name="swiglu_down_backward",
    )(og, gate, up, scores, rows, down, first, second)


def solution(mesh):
    return jax.shard_map(
        local,
        mesh=mesh,
        in_specs=(
            P(("dp", "context", "tensor"), None),
            P(("dp", "context"), "tensor"),
            P(("dp", "context"), "tensor"),
            P(("dp", "context"), None),
            P(("dp", "context", "tensor"), None),
            P("tensor", ("dp", "context")),
            P("tensor", None),
            P("tensor", ("dp", "context")),
        ),
        out_specs=(P(("dp", "context"), "tensor"), P(("dp", "context"), "tensor"), P()),
        check_vma=False,
    )
```

time: 1010 us -> 125 us (0.12)
  waiting for transfers between devices: 776 us -> 0 us
  blocking collectives: 197 us -> 0 us
  Pallas kernels: 0 us -> 115 us
  between operations: 15.3 us -> 0.68 us
  matrix products: 13.7 us -> 0 us
    psum x2 -> x0, waiting for transfers between devices: 775 us -> none  [the longest x1 668 us: local(): router_sum = lax.psum(router_part, ('dp', 'context', 'tensor'))]
    all_gather x2 -> x0, blocking collectives: 197 us -> none  [the longest x1 152 us: local(): lax.all_gather(adapter_second_factor, ('dp', 'context'), axis=1, tiled=True)]
    pallas_call x0 -> x1, Pallas kernels: none -> 115 us  [local(): pl.pallas_call(body, out_shape=(jax.ShapeDtypeStruct((256, 1024), BF), ja...]
    dot_general x5 -> x0, matrix products: 13.7 us -> none  [the longest x1 5.84 us: local(): lax.dot_general(full_grad, lax.all_gather(down_matrix, ('dp', 'context'),...]
  transfers between devices with their start and end apart: 4 -> 0, of which waited for: 2 -> 0; matrix products, arithmetic and copies ran while one was open for 1% -> 0% of each run, Pallas kernels for 0% -> 0%
where the time goes in v1:
time: 125 us; the launch traced here: 124 us
  Pallas kernels  115 us (92%)
  local copies, waits for them, and re-layouts  8.31 us (7%)
    pallas_call x1, Pallas kernels, local(): pl.pallas_call(body, out_shape=(jax.ShapeDtypeStruct((256, 1024), BF), ja...  115 us
    unnamed x18, local copies, waits for them, and re-layouts  8.31 us

profile of v1, /device:TPU:1, one launch (start us, length us, event | category | flops | bytes accessed | tf_op | source)
XLA Modules:
  0.0 124.5 jit_solution(8952435036498655811)
XLA Ops:
  0.6 0.0 copy-start.6
  0.6 0.0 copy-start.4
  0.7 0.9 copy.11.refs_3_
  1.5 0.0 copy-done.6
  1.5 0.0 copy-done.4
  1.6 0.0 copy-start
  1.6 1.2 copy-done
  2.8 0.0 copy-start.1
  2.8 1.0 copy-done.1
  3.8 0.0 copy-start.2
  3.8 1.0 copy-done.2
  4.9 0.0 copy-start.3
  4.9 0.9 copy-done.3
  5.8 0.0 copy-start.5
  5.8 0.9 copy-done.5
  6.7 115.5 %swiglu_down_backward.1 = (bf16[256,1024]{1,0:T(8,128)(2,1)S(1)}, bf16[256,1024]{1,0:T(8,128)(2,1)S(1)}, f32[8,4096]{1,0:T(8,128)S(1)}) custom-call(bf16[16,4096]{1,0:T(8,128)(2,1)S(1)} %copy-done.4, bf16[256,1024]{1,0:T(8,128)(2,1)S(1)} %copy-done.1, bf16[256,1024]{1,0:T(8,128)(2,1)S(1)} %copy-done.2, f32[256,8]{1,0:T(8,128)S(1)} %copy.11.refs_3_, ...), custom_call_target="tpu_custom_call" | custom-call | flops 3000000000 | bytes 4194304 | tf_op jit(solution)/shard_map/swiglu_down_backward/pallas_call | solution.py:450
  122.2 0.8 copy.15
  123.0 0.8 copy.16
  123.8 0.7 copy.17
Async XLA Ops:
  0.6 0.9 copy-start.6
  0.6 0.9 copy-start.4
  1.6 1.2 copy-start
  2.8 1.0 copy-start.1
  3.8 1.0 copy-start.2
  4.9 0.9 copy-start.3
  5.8 0.9 copy-start.5

commit v2 on v1

v2 whole, which is shorter than its diff:
```python
import math

import jax
import jax.numpy as jnp
from jax import lax
from jax.experimental import pallas as pl
from jax.experimental.pallas import tpu as pltpu
from jax.sharding import PartitionSpec as P

MESH = pl.DeviceIdType.MESH
NT = (((1,), (1,)), ((), ()))
BF = jnp.bfloat16
F32 = jnp.float32
HI = lax.Precision.HIGHEST
QORDER = (0, 2, 1, 3)
GSUB = 4
GW = 4096 // GSUB


def iota(shape, dim):
    return lax.broadcasted_iota(jnp.int32, shape, dim)


def kernel(
    scale,
    og_ref, gate_ref, up_ref, scores_ref, rows_ref, down_ref, first_ref, second_ref,
    gg_ref, gu_ref, rg_ref,
    wb, gb, a2b, gate, up, first, rows, hid, su, sg, rs, pd, acc, lowb, lowf,
    mid, mid_in, mid_sum, mid_got, rpb, rs_in, t1, rx, rz, fin,
    in_sem, w_send, w_recv, wz_recv,
    g_send, gsib_send, g_recv, gsib_recv,
    a2_send, a2z_recv, a2y_recv, a2x_recv,
    low_send, low_recv, m_send, m_recv,
    r_send, rs_recv, rx_recv, rz_recv, ay_recv, as_recv,
):
    dp = lax.axis_index("dp")
    y = lax.axis_index("context")
    ten = lax.axis_index("tensor")
    zh, x = dp // 4, dp % 4
    zl, c = ten // 2, ten % 2
    z = zh * 8 + zl
    oc = 1 - c

    def at_x(d):
        return (zh * 4 + (x + d + 4) % 4, y, ten)

    def at_y(d):
        return (dp, (y + d + 4) % 4, ten)

    def at_z(d):
        zz = (z + d + 16) % 16
        return ((zz // 8) * 4 + x, y, (zz % 8) * 2 + c)

    def at_zl(l):
        return (dp, y, l * 2 + c)

    sibling = (dp, y, zl * 2 + oc)

    def rc(src, dst, ss, rsm, dev):
        return pltpu.make_async_remote_copy(
            src_ref=src, dst_ref=dst, send_sem=ss, recv_sem=rsm, device_id=dev, device_id_type=MESH
        )

    def arrived(ref, sem):
        rc(ref, ref, w_send, sem, sibling).wait_recv()

    def sent(ref, sem):
        rc(ref, ref, sem, as_recv, sibling).wait_send()

    own_slot = (zh * 4 + x) * 4 + y
    my_rows = pl.ds(pl.multiple_of(ten * 16, 16), 16)

    ins = [
        pltpu.make_async_copy(og_ref, gb.at[my_rows], in_sem.at[0]),
        pltpu.make_async_copy(down_ref, wb.at[own_slot], in_sem.at[1]),
        pltpu.make_async_copy(second_ref, a2b.at[own_slot], in_sem.at[2]),
        pltpu.make_async_copy(gate_ref, gate, in_sem.at[3]),
        pltpu.make_async_copy(up_ref, up, in_sem.at[4]),
        pltpu.make_async_copy(first_ref, first, in_sem.at[5]),
        pltpu.make_async_copy(rows_ref, rows, in_sem.at[6]),
    ]
    for cp in ins:
        cp.start()

    peers = [sibling]
    peers += [(zh * 4 + (x + i) % 4, (y + j) % 4, ten) for i in range(4) for j in range(4) if i or j]
    peers += [at_z(d) for d in range(1, 16)]
    barrier = pltpu.get_barrier_semaphore()
    for dev in peers:
        pl.semaphore_signal(barrier, inc=1, device_id=dev, device_id_type=MESH)

    ins[3].wait()
    ins[4].wait()

    @pl.loop(0, 8)
    def _(i):
        r = pl.ds(pl.multiple_of(i * 32, 32), 32)
        g = gate[r, :].astype(F32)
        u = up[r, :].astype(F32)
        s = jax.nn.sigmoid(g)
        gs = g * s
        hid[r, :] = (gs * u).astype(BF)
        su[r, :] = gs
        sg[r, :] = u * s * (1.0 + g * (1.0 - s))


    p = jax.nn.sigmoid(jnp.transpose(scores_ref[...]))
    lane = iota((256, 512), 1) // 64
    scale_rows = jnp.broadcast_to(p[:, 0:1], (256, 512))
    for e in range(1, 8):
        scale_rows = jnp.where(lane == e, p[:, e : e + 1], scale_rows)
    rs[...] = scale_rows
    pd[...] = p * (1.0 - p)
    ins[5].wait()
    for n in range(2):
        cols = slice(256 * n, 256 * n + 256)
        part = jnp.dot(hid[...], first[:, cols], preferred_element_type=F32)
        for j in range(16):
            mid[j % 2, j // 2, :, cols] = part[16 * j : 16 * j + 16]
    ins[0].wait()
    ins[1].wait()
    ins[2].wait()
    ins[6].wait()
    pl.semaphore_wait(barrier, len(peers))

    def g_part(l, core, h):
        return gb.at[pl.ds(pl.multiple_of((l * 2 + core) * 16, 16), 16), pl.ds(h * GW, GW)]

    def g_block(l, core):
        return gb.at[pl.ds(pl.multiple_of((l * 2 + core) * 16, 16), 16)]

    def g_forward(l, h, to):
        rc(g_part(l, c, h), g_part(l, c, h), g_send, g_recv.at[l * GSUB + h], at_zl(to)).start()

    def g_sibling(l):
        rc(g_block(l, c), g_block(l, c), gsib_send, gsib_recv.at[l], sibling).start()

    def g_start():
        for h in range(GSUB):
            @pl.when(zl < 7)
            def _():
                g_forward(zl, h, zl + 1)

            @pl.when(zl > 0)
            def _():
                g_forward(zl, h, zl - 1)
        g_sibling(zl)

    def a2_y(zz):
        for d in (1, 2, 3):
            slot = (zz * 4 + x) * 4 + y
            rc(a2b.at[slot], a2b.at[slot], a2_send, a2y_recv.at[zz * 4 + y], at_y(d)).start()

    def a2_x(zz):
        for d in (1, 2, 3):
            slot = (zz * 4 + (x + d) % 4) * 4
            yy = (y + d) % 4
            arrived(a2b.at[(zz * 4 + x) * 4 + yy], a2y_recv.at[zz * 4 + yy])
        four = a2b.at[pl.ds((zz * 4 + x) * 4, 4)]
        for d in (1, 2, 3):
            rc(four, four, a2_send, a2x_recv.at[zz * 4 + x], at_x(d)).start()

    def a2_done(zz):
        for d in (1, 2, 3):
            xx = (x + d) % 4
            arrived(a2b.at[pl.ds((zz * 4 + xx) * 4, 4)], a2x_recv.at[zz * 4 + xx])

    zo = 1 - zh
    oth_slot = (zo * 4 + x) * 4 + y

    def a2_start():
        a2_y(zh)
        rc(a2b.at[own_slot], a2b.at[own_slot], a2_send, a2z_recv, at_z(8)).start()

    def a2_in():
        arrived(a2b.at[oth_slot], a2z_recv)
        a2_y(zo)

    def w_part(slot, q):
        return wb.at[slot, pl.ds(q * 256, 256)]

    def place(zz, q, da, db):
        xx, yy = (x + da, y + db) if q < 2 else (x + db, y + da)
        return (zz * 4 + (xx + 4) % 4) * 4 + (yy + 4) % 4

    def w_send_to(slot, q, along, d):
        first_axis_x = q < 2
        dev = at_x(d) if (along == 0) == first_axis_x else at_y(d)
        rc(w_part(slot, q), w_part(slot, q), w_send, w_recv.at[slot * 4 + q], dev).start()

    def w_wait(slot, q):
        arrived(w_part(slot, q), w_recv.at[slot * 4 + q])

    def e0(zz, q):
        s = place(zz, q, 0, 0)
        w_send_to(s, q, 0, 1)
        w_send_to(s, q, 0, -1)
        w_send_to(s, q, 1, 1)
        w_send_to(s, q, 1, -1)

    def e1(zz, q):
        for da in (-1, 1):
            s = place(zz, q, da, 0)
            w_wait(s, q)
            if da == (-1 if q % 2 == 0 else 1):
                w_send_to(s, q, 0, -da)
            w_send_to(s, q, 1, 1)
            w_send_to(s, q, 1, -1)

    def e2(zz, q):
        s = place(zz, q, 2, 0)
        w_wait(s, q)
        w_send_to(s, q, 1, 1)
        w_send_to(s, q, 1, -1)

    def e3(zz, q, das):
        for da in das:
            for db in (-1, 1):
                s = place(zz, q, da, db)
                w_wait(s, q)
                if db == (-1 if q % 2 == 0 else 1):
                    w_send_to(s, q, 1, -db)

    def e4(zz, q):
        for da in (0, -1, 1, 2):
            w_wait(place(zz, q, da, 2), q)

    def z_out(q):
        rc(w_part(own_slot, q), w_part(own_slot, q), w_send, wz_recv.at[q], at_z(8)).start()

    def z_in(q):
        arrived(w_part(oth_slot, q), wz_recv.at[q])
        e0(zo, q)

    def e13(zz, q):
        e1(zz, q)
        e3(zz, q, (0,))

    def g_step(s):
        steps = []
        for sign in (-1, 1):
            l = zl + sign * s
            ok = (l >= 0) if sign < 0 else (l <= 7)
            more = jnp.logical_and(ok, (zl < 7) if sign < 0 else (zl > 0))
            steps.append((sign, l, ok, more))
        for h in range(GSUB):
            for sign, l, ok, more in steps:
                @pl.when(ok)
                def _():
                    arrived(g_part(l, c, h), g_recv.at[l * GSUB + h])

                @pl.when(more)
                def _():
                    g_forward(l, h, zl - sign)

        for sign, l, ok, more in steps:
            @pl.when(ok)
            def _():
                g_sibling(l)

    def mid_pair():
        rc(mid.at[oc], mid_in, m_send.at[0], m_recv.at[8], sibling).start()

    def mid_out():
        arrived(mid_in, m_recv.at[8])
        mid_sum[...] = (mid[c] + mid_in[...]).astype(BF)
        for d in range(1, 8):
            l = (zl + d) % 8
            rc(mid_sum.at[l], mid_got.at[zl], m_send.at[1], m_recv.at[zl], at_zl(l)).start()
        mid_got[zl] = mid_sum[zl]

    def low_out(j, dev):
        rc(lowb.at[j], lowb.at[j], low_send, low_recv.at[j], dev).start()

    def low_own():
        a2_done(zh)
        a2_done(zo)
        for d in range(8):
            arrived(g_block(d, oc), gsib_recv.at[d])

        def low_group(i, tot):
            a = jnp.concatenate([a2b[i * 4 + k] for k in range(4)], axis=1)
            g = gb[:, pl.ds(pl.multiple_of(i * 512, 512), 512)]
            return tot + lax.dot_general(a, g, NT, preferred_element_type=F32)

        lowb[ten] = lax.fori_loop(0, 8, low_group, jnp.zeros((32, 256), F32)).astype(BF)
        for d in range(1, 8):
            low_out(ten, at_zl((zl + d) % 8))
        low_out(ten, sibling)

    def low_pass():
        for d in range(1, 8):
            j = ((zl + d) % 8) * 2 + c
            arrived(lowb.at[j], low_recv.at[j])
            low_out(j, sibling)

    def low_use():
        for d in range(8):
            j = d * 2 + oc
            arrived(lowb.at[j], low_recv.at[j])
        lowf[...] = jnp.transpose(lowb[...].reshape(512, 256).astype(F32))
        for d in range(1, 8):
            l = (zl + d) % 8
            arrived(mid_got.at[l], m_recv.at[l])
        middle = mid_got[0].astype(F32)
        for l in range(1, 8):
            middle = middle + mid_got[l].astype(F32)
        prod = middle * lowf[my_rows]
        spread = jnp.where(iota((8, 512), 1) // 64 == iota((8, 512), 0), 1.0, 0.0)
        eye = jnp.where(iota((8, 8), 0) == iota((8, 8), 1), 1.0, 0.0)
        probs = lax.dot_general(spread, prod, NT, precision=HI, preferred_element_type=F32)
        slope = lax.dot_general(eye, pd[my_rows], NT, precision=HI, preferred_element_type=F32)
        logits = probs * slope
        for k in range(4):
            part = jnp.dot(
                logits, rows[:, 1024 * k : 1024 * k + 1024].astype(F32), precision=HI, preferred_element_type=F32
            )
            for i in range(8):
                rpb[k * 8 + i] = part[:, 128 * i : 128 * i + 128]
        rc(rpb.at[pl.ds(oc * 16, 16)], rs_in, r_send.at[0], rs_recv, sibling).start()
        hid[:, 0:512] = (lowf[...] * rs[...]).astype(BF)

    def low_rank_term():
        for n in range(4):
            acc[:, 256 * n : 256 * n + 256] += lax.dot_general(
                hid[:, 0:512], first[256 * n : 256 * n + 256, :], NT, preferred_element_type=F32
            )

    def base_tile(zz, n):
        tot = None
        for k in range(4):
            w = jnp.concatenate(
                [wb[zz * 16 + k * 4 + i, pl.ds(n * 256, 256), :] for i in range(4)], axis=1
            )
            g = gb[:, pl.ds(pl.multiple_of(zz * 2048 + k * 512, 512), 512)]
            t = lax.dot_general(g, w, NT, preferred_element_type=F32)
            tot = t if tot is None else tot + t
        return tot

    def base_own(q):
        e4(zh, q)
        acc[:, 256 * q : 256 * q + 256] = base_tile(zh, q)

    def base_other(q):
        e4(zo, q)
        cols = slice(256 * q, 256 * q + 256)
        hg = acc[:, cols] + base_tile(zo, q)
        gu_ref[:, cols] = (hg * su[:, cols]).astype(BF)
        gg_ref[:, cols] = (hg * sg[:, cols]).astype(BF)

    here = x * 4 + y
    piece = c * 16 + here
    around = [(dx, dy) for dx in range(4) for dy in range(4) if dx or dy]

    def at_xy(dx, dy):
        return (zh * 4 + (x + dx) % 4, (y + dy) % 4, ten)

    def place_xy(dx, dy):
        return ((x + dx) % 4) * 4 + (y + dy) % 4

    def router_p():
        arrived(rs_in, rs_recv)
        t1[...] = rpb[pl.ds(c * 16, 16)] + rs_in[...]
        for d in around:
            rc(t1.at[place_xy(*d)], rx.at[here], r_send.at[1], rx_recv.at[here], at_xy(*d)).start()
        rx[here] = t1[here]

    def router_z():
        for d in around:
            arrived(rx.at[place_xy(*d)], rx_recv.at[place_xy(*d)])
        tot = rx[0]
        for l in range(1, 16):
            tot = tot + rx[l]
        rz[z] = tot
        for d in range(1, 16):
            rc(rz.at[z], rz.at[z], r_send.at[2], rz_recv.at[z], at_z(d)).start()

    def router_back_p():
        for d in range(1, 16):
            zz = (z + d) % 16
            arrived(rz.at[zz], rz_recv.at[zz])
        tot = rz[0]
        for l in range(1, 16):
            tot = tot + rz[l]
        fin[piece] = tot / scale
        for d in around:
            rc(fin.at[piece], fin.at[piece], r_send.at[3], ay_recv.at[here], at_xy(*d)).start()

    def router_back():
        for d in around:
            arrived(fin.at[c * 16 + place_xy(*d)], ay_recv.at[place_xy(*d)])
        half = fin.at[pl.ds(c * 16, 16)]
        rc(half, half, r_send.at[4], as_recv, sibling).start()

    def router_end():
        arrived(fin.at[pl.ds(oc * 16, 16)], as_recv)
        for i in range(32):
            rg_ref[:, 128 * i : 128 * i + 128] = fin[i]

    g_start()
    a2_start()
    mid_pair()
    e0(zh,0)
    e0(zh,2)
    e0(zh,1)
    e0(zh,3)
    g_step(1)
    a2_x(zh)
    e13(zh,0)
    e13(zh,2)
    g_step(2)
    e13(zh,1)
    e13(zh,3)
    g_step(3)
    e2(zh,0)
    e2(zh,2)
    a2_in()
    g_step(4)
    e2(zh,1)
    e2(zh,3)
    a2_x(zo)
    g_step(5)
    mid_out()
    e3(zh,0,(-1,1))
    e3(zh,2,(-1,1))
    e3(zh,1,(-1,1))
    e3(zh,3,(-1,1))
    g_step(6)
    z_out(0)
    e3(zh,0,(2,))
    e3(zh,2,(2,))
    g_step(7)
    z_out(2)
    e3(zh,1,(2,))
    e3(zh,3,(2,))
    low_own()
    z_out(1)
    base_own(0)
    base_own(2)
    base_own(1)
    base_own(3)
    low_pass()
    low_use()
    z_out(3)
    z_in(0)
    z_in(2)
    router_p()
    e13(zo,0)
    e13(zo,2)
    router_z()
    z_in(1)
    e2(zo,0)
    e2(zo,2)
    e3(zo,0,(-1,1))
    e3(zo,2,(-1,1))
    z_in(3)
    e13(zo,1)
    e13(zo,3)
    e3(zo,0,(2,))
    e3(zo,2,(2,))
    low_rank_term()
    router_back_p()
    e2(zo,1)
    e2(zo,3)
    e3(zo,1,(-1,1))
    e3(zo,3,(-1,1))
    router_back()
    base_other(0)
    base_other(2)
    e3(zo,1,(2,))
    e3(zo,3,(2,))
    router_end()
    base_other(1)
    base_other(3)

    sent(wb.at[pl.ds(0, 31)], w_send)
    sent(gb.at[pl.ds(0, 128)], gsib_send)
    inner = jnp.logical_and(zl > 0, zl < 7)

    @pl.when(inner)
    def _():
        sent(gb.at[pl.ds(0, 144)], g_send)

    @pl.when(jnp.logical_not(inner))
    def _():
        sent(gb.at[pl.ds(0, 16)], g_send)

    sent(a2b.at[pl.ds(0, 31)], a2_send)
    sent(lowb.at[pl.ds(0, 15)], low_send)
    sent(mid_in, m_send.at[0])
    sent(mid_sum.at[pl.ds(0, 7)], m_send.at[1])
    for i, n in enumerate((16, 15, 15, 15, 16)):
        sent(rpb.at[pl.ds(0, n)], r_send.at[i])


def local(og, gate, up, scores, rows, down, first, second):
    tokens = gate.shape[0] * lax.axis_size("dp") * lax.axis_size("context")
    anywhere = pl.BlockSpec(memory_space=pl.ANY)
    vmem = pl.BlockSpec(memory_space=pltpu.VMEM)
    dma = pltpu.SemaphoreType.DMA
    V = pltpu.VMEM

    def body(*refs):
        kernel(math.sqrt(tokens), *refs)

    return pl.pallas_call(
        body,
        out_shape=(
            jax.ShapeDtypeStruct((256, 1024), BF),
            jax.ShapeDtypeStruct((256, 1024), BF),
            jax.ShapeDtypeStruct((8, 4096), F32),
        ),
        in_specs=[anywhere, anywhere, anywhere, vmem, anywhere, anywhere, anywhere, anywhere],
        out_specs=(vmem, vmem, vmem),
        scratch_shapes=[
            V((32, 1024, 128), BF), V((256, 4096), BF), V((32, 32, 128), BF),
            V((256, 1024), BF), V((256, 1024), BF), V((1024, 512), BF), V((16, 4096), BF),
            V((256, 1024), BF), V((256, 1024), F32), V((256, 1024), F32), V((256, 512), F32),
            V((256, 8), F32), V((256, 1024), F32), V((16, 32, 256), BF), V((256, 512), F32),
            V((2, 8, 16, 512), F32), V((8, 16, 512), F32), V((8, 16, 512), BF), V((8, 16, 512), BF),
            V((32, 8, 128), F32), V((16, 8, 128), F32), V((16, 8, 128), F32), V((16, 8, 128), F32),
            V((16, 8, 128), F32), V((32, 8, 128), F32),
            dma((7,)), dma, dma((128,)), dma((4,)),
            dma, dma, dma((8 * GSUB,)), dma((8,)),
            dma, dma, dma((8,)), dma((8,)),
            dma, dma((16,)), dma((2,)), dma((9,)),
            dma((5,)), dma, dma((16,)), dma((16,)), dma((16,)), dma,
        ],
        compiler_params=pltpu.CompilerParams(
            collective_id=0, has_side_effects=True, vmem_limit_bytes=62 * 2**20
        ),
        cost_estimate=pl.CostEstimate(flops=3 * 10**9, bytes_accessed=4 * 2**20, transcendentals=2**18),
        name="swiglu_down_backward",
    )(og, gate, up, jnp.transpose(scores), rows, down, first, second)


def solution(mesh):
    return jax.shard_map(
        local,
        mesh=mesh,
        in_specs=(
            P(("dp", "context", "tensor"), None),
            P(("dp", "context"), "tensor"),
            P(("dp", "context"), "tensor"),
            P(("dp", "context"), None),
            P(("dp", "context", "tensor"), None),
            P("tensor", ("dp", "context")),
            P("tensor", None),
            P("tensor", ("dp", "context")),
        ),
        out_specs=(P(("dp", "context"), "tensor"), P(("dp", "context"), "tensor"), P()),
        check_vma=False,
    )
```

time: 125 us -> 108 us (0.86)
  Pallas kernels: 115 us -> 104 us
  local copies, waits for them, and re-layouts: 8.31 us -> 3.61 us
    pallas_call x1, Pallas kernels: 115 us -> 104 us  [local(): pl.pallas_call(body, out_shape=(jax.ShapeDtypeStruct((256, 1024), BF), ja...]
    unnamed x18 -> x7, local copies, waits for them, and re-layouts: 8.31 us -> 3.61 us
where the time goes in v2:
time: 108 us
  Pallas kernels  104 us (96%)
  local copies, waits for them, and re-layouts  3.61 us (3%)
    pallas_call x1, Pallas kernels, local(): pl.pallas_call(body, out_shape=(jax.ShapeDtypeStruct((256, 1024), BF), ja...  104 us
    unnamed x7, local copies, waits for them, and re-layouts  3.61 us

profile of v2, /device:TPU:1, one launch (start us, length us, event | category | flops | bytes accessed | tf_op | source)
XLA Modules:
  0.0 107.9 jit_solution(17571140936453230950)
XLA Ops:
  0.6 103.6 %swiglu_down_backward.1 = (bf16[256,1024]{1,0:T(8,128)(2,1)}, bf16[256,1024]{1,0:T(8,128)(2,1)}, f32[8,4096]{1,0:T(8,128)}) custom-call(bf16[16,4096]{1,0:T(8,128)(2,1)} %refs_0_.1, bf16[256,1024]{1,0:T(8,128)(2,1)} %refs_1_.1, bf16[256,1024]{1,0:T(8,128)(2,1)} %refs_2_.1, f32[8,256]{1,0:T(8,128)} %bitcast.1, bf16[16,4096]{1,0:T(8,128)(2,1)} %refs_4_.1, ...), custom_call_target="tpu_custom_call" | custom-call | flops 3000000000 | bytes 4194304 | tf_op jit(solution)/shard_map/swiglu_down_backward/pallas_call | solution.py:506
  104.3 0.0 copy-start
  104.3 1.9 %copy.14 = bf16[256,1024]{1,0:T(8,128)(2,1)} copy(bf16[256,1024]{1,0:T(8,128)(2,1)} %get-tuple-element.6) | data formatting | bytes 1048576
  106.2 0.0 copy-done
  106.2 0.0 copy-start.1
  106.2 0.8 copy.15
  107.0 0.2 copy-done.1
  107.2 0.7 copy.16
Async XLA Ops:
  104.3 1.9 %copy-start = (bf16[256,1024]{1,0:T(8,128)(2,1)S(1)}, bf16[256,1024]{1,0:T(8,128)(2,1)}, u32[]{:S(2)}) copy-start(bf16[256,1024]{1,0:T(8,128)(2,1)} %get-tuple-element.7) | copy-start | bytes 1572868
  106.2 1.0 copy-start.1

commit v3 on v2

--- a/solution.py
+++ b/solution.py
@@ -25,11 +25,11 @@
     scale,
     og_ref, gate_ref, up_ref, scores_ref, rows_ref, down_ref, first_ref, second_ref,
     gg_ref, gu_ref, rg_ref,
-    wb, gb, a2b, gate, up, first, rows, hid, su, sg, rs, pd, acc, lowb, lowf,
+    wb, gb, a2l, gs, gx, lp, lr, gate, up, first, rows, hid, su, sg, rs, pd, acc, lowb,
     mid, mid_in, mid_sum, mid_got, rpb, rs_in, t1, rx, rz, fin,
     in_sem, w_send, w_recv, wz_recv,
     g_send, gsib_send, g_recv, gsib_recv,
-    a2_send, a2z_recv, a2y_recv, a2x_recv,
+    a2z_send, a2z_recv, a2_send, a2_recv, gx_send, gx_recv, lp_send, lp_recv,
     low_send, low_recv, m_send, m_recv,
     r_send, rs_recv, rx_recv, rz_recv, ay_recv, as_recv,
 ):
@@ -73,7 +73,7 @@
     ins = [
         pltpu.make_async_copy(og_ref, gb.at[my_rows], in_sem.at[0]),
         pltpu.make_async_copy(down_ref, wb.at[own_slot], in_sem.at[1]),
-        pltpu.make_async_copy(second_ref, a2b.at[own_slot], in_sem.at[2]),
+        pltpu.make_async_copy(second_ref, a2l.at[ten, zh], in_sem.at[2]),
         pltpu.make_async_copy(gate_ref, gate, in_sem.at[3]),
         pltpu.make_async_copy(up_ref, up, in_sem.at[4]),
         pltpu.make_async_copy(first_ref, first, in_sem.at[5]),
@@ -146,35 +146,60 @@
                 g_forward(zl, h, zl - 1)
         g_sibling(zl)
 
-    def a2_y(zz):
-        for d in (1, 2, 3):
-            slot = (zz * 4 + x) * 4 + y
-            rc(a2b.at[slot], a2b.at[slot], a2_send, a2y_recv.at[zz * 4 + y], at_y(d)).start()
-
-    def a2_x(zz):
-        for d in (1, 2, 3):
-            slot = (zz * 4 + (x + d) % 4) * 4
-            yy = (y + d) % 4
-            arrived(a2b.at[(zz * 4 + x) * 4 + yy], a2y_recv.at[zz * 4 + yy])
-        four = a2b.at[pl.ds((zz * 4 + x) * 4, 4)]
-        for d in (1, 2, 3):
-            rc(four, four, a2_send, a2x_recv.at[zz * 4 + x], at_x(d)).start()
-
-    def a2_done(zz):
-        for d in (1, 2, 3):
-            xx = (x + d) % 4
-            arrived(a2b.at[pl.ds((zz * 4 + xx) * 4, 4)], a2x_recv.at[zz * 4 + xx])
+    here = x * 4 + y
+    piece = c * 16 + here
+    around = [(dx, dy) for dx in range(4) for dy in range(4) if dx or dy]
+
+    def at_xy(dx, dy):
+        return (zh * 4 + (x + dx) % 4, (y + dy) % 4, ten)
+
+    def place_xy(dx, dy):
+        return ((x + dx) % 4) * 4 + (y + dy) % 4
 
     zo = 1 - zh
     oth_slot = (zo * 4 + x) * 4 + y
 
-    def a2_start():
-        a2_y(zh)
-        rc(a2b.at[own_slot], a2b.at[own_slot], a2_send, a2z_recv, at_z(8)).start()
-
-    def a2_in():
-        arrived(a2b.at[oth_slot], a2z_recv)
-        a2_y(zo)
+    def a2_z():
+        rc(a2l.at[ten, zh], a2l.at[ten, zh], a2z_send, a2z_recv, at_z(8)).start()
+
+    def a2_out(j, dev):
+        rc(a2l.at[j], a2l.at[j], a2_send, a2_recv.at[j], dev).start()
+
+    def a2_line():
+        arrived(a2l.at[ten, zo], a2z_recv)
+        for d in range(1, 8):
+            a2_out(ten, at_zl((zl + d) % 8))
+        a2_out(ten, sibling)
+
+    def a2_pass():
+        for d in range(1, 8):
+            j = ((zl + d) % 8) * 2 + c
+            arrived(a2l.at[j], a2_recv.at[j])
+            a2_out(j, sibling)
+
+    def gx_out():
+        block = gb[my_rows, :]
+        for i in range(16):
+            for k in range(2):
+                s = (k * 16 + i) * 128
+                gs[i, k] = block[:, s : s + 128]
+        for d in around:
+            rc(gs.at[place_xy(*d)], gx.at[here], gx_send, gx_recv.at[here], at_xy(*d)).start()
+        gx[here] = gs[here]
+
+    def low_part():
+        for d in around:
+            arrived(gx.at[place_xy(*d)], gx_recv.at[place_xy(*d)])
+        for l in range(8):
+            arrived(a2l.at[l * 2 + oc], a2_recv.at[l * 2 + oc])
+        g = jnp.concatenate([gx[:, k].reshape(256, 128) for k in range(2)], axis=1)
+        for n in range(2):
+            a = jnp.concatenate([a2l[8 * n : 8 * n + 8, k].reshape(256, 128) for k in range(2)], axis=1)
+            r = lax.dot_general(g, a, NT, preferred_element_type=F32)
+            lp[:, :, 256 * n : 256 * n + 256] = r.reshape(16, 16, 256)
+        for d in around:
+            rc(lp.at[place_xy(*d)], lr.at[here], lp_send, lp_recv.at[here], at_xy(*d)).start()
+        lr[here] = lp[here]
 
     def w_part(slot, q):
         return wb.at[slot, pl.ds(q * 256, 256)]
@@ -272,40 +297,24 @@
     def low_out(j, dev):
         rc(lowb.at[j], lowb.at[j], low_send, low_recv.at[j], dev).start()
 
-    def low_own():
-        a2_done(zh)
-        a2_done(zo)
-        for d in range(8):
-            arrived(g_block(d, oc), gsib_recv.at[d])
-
-        def low_group(i, tot):
-            a = jnp.concatenate([a2b[i * 4 + k] for k in range(4)], axis=1)
-            g = gb[:, pl.ds(pl.multiple_of(i * 512, 512), 512)]
-            return tot + lax.dot_general(a, g, NT, preferred_element_type=F32)
-
-        lowb[ten] = lax.fori_loop(0, 8, low_group, jnp.zeros((32, 256), F32)).astype(BF)
+    def low_sum():
+        for d in around:
+            arrived(lr.at[place_xy(*d)], lp_recv.at[place_xy(*d)])
+        tot = lr[0]
+        for l in range(1, 16):
+            tot = tot + lr[l]
+        own = tot.astype(BF)
+        lowb[ten] = own
         for d in range(1, 8):
             low_out(ten, at_zl((zl + d) % 8))
         low_out(ten, sibling)
-
-    def low_pass():
-        for d in range(1, 8):
-            j = ((zl + d) % 8) * 2 + c
-            arrived(lowb.at[j], low_recv.at[j])
-            low_out(j, sibling)
-
-    def low_use():
-        for d in range(8):
-            j = d * 2 + oc
-            arrived(lowb.at[j], low_recv.at[j])
-        lowf[...] = jnp.transpose(lowb[...].reshape(512, 256).astype(F32))
         for d in range(1, 8):
             l = (zl + d) % 8
             arrived(mid_got.at[l], m_recv.at[l])
         middle = mid_got[0].astype(F32)
         for l in range(1, 8):
             middle = middle + mid_got[l].astype(F32)
-        prod = middle * lowf[my_rows]
+        prod = middle * own.astype(F32)
         spread = jnp.where(iota((8, 512), 1) // 64 == iota((8, 512), 0), 1.0, 0.0)
         eye = jnp.where(iota((8, 8), 0) == iota((8, 8), 1), 1.0, 0.0)
         probs = lax.dot_general(spread, prod, NT, precision=HI, preferred_element_type=F32)
@@ -318,7 +327,23 @@
             for i in range(8):
                 rpb[k * 8 + i] = part[:, 128 * i : 128 * i + 128]
         rc(rpb.at[pl.ds(oc * 16, 16)], rs_in, r_send.at[0], rs_recv, sibling).start()
-        hid[:, 0:512] = (lowf[...] * rs[...]).astype(BF)
+
+    def low_pass():
+        for d in range(1, 8):
+            j = ((zl + d) % 8) * 2 + c
+            arrived(lowb.at[j], low_recv.at[j])
+            low_out(j, sibling)
+
+    def low_use():
+        for d in range(8):
+            j = d * 2 + oc
+            arrived(lowb.at[j], low_recv.at[j])
+        low = lowb[...].reshape(256, 512).astype(F32)
+        hid[:, 0:512] = (low * rs[...]).astype(BF)
+
+    def g_done():
+        for d in range(8):
+            arrived(g_block(d, oc), gsib_recv.at[d])
 
     def low_rank_term():
         for n in range(4):
@@ -348,16 +373,6 @@
         gu_ref[:, cols] = (hg * su[:, cols]).astype(BF)
         gg_ref[:, cols] = (hg * sg[:, cols]).astype(BF)
 
-    here = x * 4 + y
-    piece = c * 16 + here
-    around = [(dx, dy) for dx in range(4) for dy in range(4) if dx or dy]
-
-    def at_xy(dx, dy):
-        return (zh * 4 + (x + dx) % 4, (y + dy) % 4, ten)
-
-    def place_xy(dx, dy):
-        return ((x + dx) % 4) * 4 + (y + dy) % 4
-
     def router_p():
         arrived(rs_in, rs_recv)
         t1[...] = rpb[pl.ds(c * 16, 16)] + rs_in[...]
@@ -397,81 +412,83 @@
         for i in range(32):
             rg_ref[:, 128 * i : 128 * i + 128] = fin[i]
 
-    g_start()
-    a2_start()
+    a2_z()
+    gx_out()
+    z_out(0)
+    z_out(2)
+    z_out(1)
+    z_out(3)
     mid_pair()
     e0(zh,0)
     e0(zh,2)
     e0(zh,1)
     e0(zh,3)
-    g_step(1)
-    a2_x(zh)
     e13(zh,0)
     e13(zh,2)
-    g_step(2)
+    a2_line()
     e13(zh,1)
     e13(zh,3)
-    g_step(3)
     e2(zh,0)
     e2(zh,2)
-    a2_in()
-    g_step(4)
     e2(zh,1)
     e2(zh,3)
-    a2_x(zo)
-    g_step(5)
-    mid_out()
+    g_start()
     e3(zh,0,(-1,1))
     e3(zh,2,(-1,1))
     e3(zh,1,(-1,1))
     e3(zh,3,(-1,1))
-    g_step(6)
-    z_out(0)
+    mid_out()
+    a2_pass()
     e3(zh,0,(2,))
     e3(zh,2,(2,))
-    g_step(7)
-    z_out(2)
     e3(zh,1,(2,))
     e3(zh,3,(2,))
-    low_own()
-    z_out(1)
-    base_own(0)
-    base_own(2)
-    base_own(1)
-    base_own(3)
-    low_pass()
-    low_use()
-    z_out(3)
+    low_part()
+    g_step(1)
     z_in(0)
     z_in(2)
-    router_p()
+    low_sum()
+    z_in(1)
+    z_in(3)
     e13(zo,0)
     e13(zo,2)
-    router_z()
-    z_in(1)
+    g_step(2)
+    router_p()
+    e13(zo,1)
+    e13(zo,3)
+    g_step(3)
     e2(zo,0)
     e2(zo,2)
+    e2(zo,1)
+    e2(zo,3)
+    router_z()
+    g_step(4)
     e3(zo,0,(-1,1))
     e3(zo,2,(-1,1))
-    z_in(3)
-    e13(zo,1)
-    e13(zo,3)
+    e3(zo,1,(-1,1))
+    e3(zo,3,(-1,1))
+    low_pass()
+    g_step(5)
     e3(zo,0,(2,))
     e3(zo,2,(2,))
+    e3(zo,1,(2,))
+    e3(zo,3,(2,))
+    g_step(6)
+    low_use()
+    g_step(7)
+    router_back_p()
+    g_done()
+    base_own(0)
+    base_own(1)
+    base_own(2)
+    base_own(3)
     low_rank_term()
-    router_back_p()
-    e2(zo,1)
-    e2(zo,3)
-    e3(zo,1,(-1,1))
-    e3(zo,3,(-1,1))
     router_back()
     base_other(0)
+    base_other(1)
     base_other(2)
-    e3(zo,1,(2,))
-    e3(zo,3,(2,))
+    base_other(3)
     router_end()
-    base_other(1)
-    base_other(3)
 
     sent(wb.at[pl.ds(0, 31)], w_send)
     sent(gb.at[pl.ds(0, 128)], gsib_send)
@@ -485,7 +502,10 @@
     def _():
         sent(gb.at[pl.ds(0, 16)], g_send)
 
-    sent(a2b.at[pl.ds(0, 31)], a2_send)
+    sent(a2l.at[0, 0], a2z_send)
+    sent(a2l.at[pl.ds(0, 15)], a2_send)
+    sent(gs.at[pl.ds(0, 15)], gx_send)
+    sent(lp.at[pl.ds(0, 15)], lp_send)
     sent(lowb.at[pl.ds(0, 15)], low_send)
     sent(mid_in, m_send.at[0])
     sent(mid_sum.at[pl.ds(0, 7)], m_send.at[1])
@@ -513,16 +533,17 @@
         in_specs=[anywhere, anywhere, anywhere, vmem, anywhere, anywhere, anywhere, anywhere],
         out_specs=(vmem, vmem, vmem),
         scratch_shapes=[
-            V((32, 1024, 128), BF), V((256, 4096), BF), V((32, 32, 128), BF),
+            V((32, 1024, 128), BF), V((256, 4096), BF), V((16, 2, 32, 128), BF),
+            V((16, 2, 16, 128), BF), V((16, 2, 16, 128), BF), V((16, 16, 512), F32), V((16, 16, 512), F32),
             V((256, 1024), BF), V((256, 1024), BF), V((1024, 512), BF), V((16, 4096), BF),
             V((256, 1024), BF), V((256, 1024), F32), V((256, 1024), F32), V((256, 512), F32),
-            V((256, 8), F32), V((256, 1024), F32), V((16, 32, 256), BF), V((256, 512), F32),
+            V((256, 8), F32), V((256, 1024), F32), V((16, 16, 512), BF),
             V((2, 8, 16, 512), F32), V((8, 16, 512), F32), V((8, 16, 512), BF), V((8, 16, 512), BF),
             V((32, 8, 128), F32), V((16, 8, 128), F32), V((16, 8, 128), F32), V((16, 8, 128), F32),
             V((16, 8, 128), F32), V((32, 8, 128), F32),
             dma((7,)), dma, dma((128,)), dma((4,)),
             dma, dma, dma((8 * GSUB,)), dma((8,)),
-            dma, dma, dma((8,)), dma((8,)),
+            dma, dma, dma, dma((16,)), dma, dma((16,)), dma, dma((16,)),
             dma, dma((16,)), dma((2,)), dma((9,)),
             dma((5,)), dma, dma((16,)), dma((16,)), dma((16,)), dma,
         ],

time: 108 us -> 103 us (0.954)
  Pallas kernels: 104 us -> 98.8 us
    pallas_call x1, Pallas kernels: 104 us -> 98.8 us  [local(): pl.pallas_call(body, out_shape=(jax.ShapeDtypeStruct((256, 1024), BF), ja...]
where the time goes in v3:
time: 103 us
  Pallas kernels  98.8 us (96%)
  local copies, waits for them, and re-layouts  3.61 us (4%)
    pallas_call x1, Pallas kernels, local(): pl.pallas_call(body, out_shape=(jax.ShapeDtypeStruct((256, 1024), BF), ja...  98.8 us
    unnamed x7, local copies, waits for them, and re-layouts  3.61 us

profile of v3, /device:TPU:1, one launch (start us, length us, event | category | flops | bytes accessed | tf_op | source)
XLA Modules:
  0.0 103.1 jit_solution(1829422099152188676)
XLA Ops:
  0.6 98.8 %swiglu_down_backward.1 = (bf16[256,1024]{1,0:T(8,128)(2,1)}, bf16[256,1024]{1,0:T(8,128)(2,1)}, f32[8,4096]{1,0:T(8,128)}) custom-call(bf16[16,4096]{1,0:T(8,128)(2,1)} %refs_0_.1, bf16[256,1024]{1,0:T(8,128)(2,1)} %refs_1_.1, bf16[256,1024]{1,0:T(8,128)(2,1)} %refs_2_.1, f32[8,256]{1,0:T(8,128)} %bitcast.1, bf16[16,4096]{1,0:T(8,128)(2,1)} %refs_4_.1, ...), custom_call_target="tpu_custom_call" | custom-call | flops 3000000000 | bytes 4194304 | tf_op jit(solution)/shard_map/swiglu_down_backward/pallas_call | solution.py:526
  99.5 0.0 copy-start
  99.5 1.9 %copy.14 = bf16[256,1024]{1,0:T(8,128)(2,1)} copy(bf16[256,1024]{1,0:T(8,128)(2,1)} %get-tuple-element.6) | data formatting | bytes 1048576
  101.4 0.0 copy-done
  101.4 0.0 copy-start.1
  101.4 0.8 copy.15
  102.2 0.2 copy-done.1
  102.4 0.7 copy.16
Async XLA Ops:
  99.5 1.9 %copy-start = (bf16[256,1024]{1,0:T(8,128)(2,1)S(1)}, bf16[256,1024]{1,0:T(8,128)(2,1)}, u32[]{:S(2)}) copy-start(bf16[256,1024]{1,0:T(8,128)(2,1)} %get-tuple-element.7) | copy-start | bytes 1572868
  101.4 1.0 copy-start.1
